TPU v7x, 128 devices: a whole 4x4x4 slice. The times are simulated.
128 devices in a mesh: blk: 32 (over x, y, z_hi), head: 4 (over z_lo, core).
Axes of the slice: x: 4, y: 4, z: 4 (z_hi: 2, z_lo: 2; z = z_hi * 2 + z_lo), core: 2. Of those that a mesh axis runs over, the one named last changes fastest.
Arguments:
- x_video: bfloat16 [16384, 3072], P(('blk', 'head')), may hold values from -6 to 6
- x_text: bfloat16 [256, 3072], replicated, may hold values from -6 to 6
- w_qkv_video: bfloat16 [3072, 3, 1536], P(None, None, 'head'), may hold values from -0.109375 to 0.109375
- w_qkv_text: bfloat16 [3072, 3, 1536], P(None, None, 'head'), may hold values from -0.109375 to 0.109375
- w_out_video: bfloat16 [1536, 3072], P('head'), may hold values from -0.15625 to 0.15625
- w_out_text: bfloat16 [1536, 3072], P('head'), may hold values from -0.15625 to 0.15625
- qk_gains: float32 [4, 128], replicated, may hold values from 0.8 to 1.4
- modulation: float32 [50, 6, 3072], replicated, may hold values from -3 to 3
- text_len: int32 [1], replicated, may hold values from 64 to 256
- timestep: int32 [1], replicated, may hold values from 0 to 49
Outputs:
- video_out: bfloat16 [16384, 3072], P(('blk', 'head'))
- text_out: bfloat16 [256, 3072], P('head')
All inputs are finite; a program needn't handle non-finite values.
Results may differ from a plain program's by a relative error of at most 0.0052.
Values may be sent and summed in bfloat16 or wider, within the bound.
A program may use at most 192 MiB of HBM per device.

v0:
```python
import functools
import math

import jax
import jax.numpy as jnp
from jax import lax
from jax.experimental import pallas as pl
from jax.experimental.pallas import tpu as pltpu
from jax.sharding import Mesh, PartitionSpec as P

AXES = ("x", "y", "zh", "zl", "c")
MESH = pl.DeviceIdType.MESH
BF16, F32 = jnp.bfloat16, jnp.float32
D = 3072
HD = 128
NH = 3
W = NH * HD
HALF = 256
TXT = 256
TQ = 32
QROWS = 8 * HALF + TQ
ORDER = (3, 1, 2, 0)
CH = 768
NCH = D // CH
EXP_SCALE = math.log2(math.e) / math.sqrt(HD)
VMEM_LIMIT = 60 << 20


def coords():
    x, y, zh, zl, c = (lax.axis_index(a) for a in AXES)
    return x, y, zh * 2 + zl, c


def dev(x, y, z, c):
    z = lax.rem(z + 4, 4)
    return (lax.rem(x + 4, 4), lax.rem(y + 4, 4), z // 2, lax.rem(z, 2), c)


class Sends:
    def __init__(self, sems, peer):
        self.sems, self.peer, self.count, self.pending = sems, peer, 0, []

    def start(self, src, dst, recv_sem, device, pred=None):
        slot = self.count
        self.count += 1
        get = src if callable(src) else (lambda: src)

        pltpu.make_async_remote_copy(
            src_ref=get(), dst_ref=dst, send_sem=self.sems.at[slot], recv_sem=recv_sem,
            device_id=device, device_id_type=MESH).start()

        def wait():
            pltpu.make_async_remote_copy(
                src_ref=get(), dst_ref=get(), send_sem=self.sems.at[slot], recv_sem=self.sems.at[slot],
                device_id=self.peer, device_id_type=MESH).wait_send()

        self.pending.append((pred, wait))

    def finish(self):
        for pred, wait in self.pending:
            if pred is None:
                wait()
            else:
                pl.when(pred)(wait)


def signal(sem, device):
    pl.semaphore_signal(sem, inc=1, device_id=device, device_id_type=MESH)


def norm_rows(src, dst, dst_row, count, shift, scale1):
    def strip(i, carry):
        wide = src[pl.ds(pl.multiple_of(i * 16, 16), 16), :].astype(F32)
        centred = wide - jnp.mean(wide, axis=-1, keepdims=True)
        variance = jnp.mean(centred * centred, axis=-1, keepdims=True)
        out = centred * lax.rsqrt(variance + 1e-06) * scale1 + shift
        dst[pl.ds(pl.multiple_of(dst_row + i * 16, 16), 16), :] = out.astype(BF16)
        return carry

    lax.fori_loop(0, count // 16, strip, 0, unroll=2)


def project(rows, weights, outs, gain_query, gain_key):
    for part in range(3):
        flat = jnp.dot(rows, weights[part][...], preferred_element_type=F32)
        for h in range(NH):
            lanes = slice(h * HD, (h + 1) * HD)
            u = flat[:, lanes]
            if part < 2:
                gain = gain_query if part == 0 else gain_key
                meansq = jnp.mean(u * u, axis=-1, keepdims=True)
                u = u * lax.rsqrt(meansq + 1e-06) * gain
            outs[part][:, lanes] = u.astype(BF16)


def project_wide(rows, weight, out, gain_query, gain_key):
    flat = jnp.dot(rows, weight[...], preferred_element_type=F32)
    for part in range(3):
        for h in range(NH):
            u = flat[:, part * W + h * HD : part * W + (h + 1) * HD]
            if part < 2:
                gain = gain_query if part == 0 else gain_key
                meansq = jnp.mean(u * u, axis=-1, keepdims=True)
                u = u * lax.rsqrt(meansq + 1e-06) * gain
            out[part, :, h * HD : (h + 1) * HD] = u.astype(BF16)


def attend(qb, q0, count, keys, values, acc, first, mask=None):
    for h in range(NH):
        lanes = slice(h * HD, (h + 1) * HD)
        query = qb[pl.ds(q0, count), lanes]
        total = None
        for key_ref, value_ref in zip(keys, values):
            scores = lax.dot_general(
                query, key_ref[:, lanes], (((1,), (1,)), ((), ())), preferred_element_type=F32)
            expo = jnp.exp2(scores * EXP_SCALE)
            if mask is not None:
                expo = jnp.where(mask, expo, 0.0)
            value = value_ref[:, lanes]
            wide = jnp.concatenate([value, jnp.ones_like(value)], axis=1)
            part = jnp.dot(expo.astype(BF16), wide, preferred_element_type=F32)
            total = part if total is None else total + part
        if first:
            acc[h, pl.ds(q0, count), :] = total
        else:
            acc[h, pl.ds(q0, count), :] += total


def coded_denoms(acc, rows):
    parts = [acc[h, rows, HD:] for h in range(NH)]
    lane = lax.broadcasted_iota(jnp.int32, parts[0].shape, 1)
    return jnp.where(lane < 8, parts[0], jnp.where(lane < 16, parts[1], parts[2]))


def q_row(pos, half):
    return TQ + ORDER.index(pos) * HALF + (0 if half else 4 * HALF)


TROW = 0


def block_kernel(x_ref, xt_ref, wv_ref, wt_ref, mod_ref, gains_ref, wov_ref, wot_ref, len_ref, step_ref,
                 video_out_ref, text_out_ref, wst_ref,
                 xb, xtb, wvb, wtb, mod0, mod1, mod2, nb, stg, tqst, qb, kvb, tkv, acc, osend, dsend, orecv, drecv,
                 rrecv, rden, tsend, tden, trecv, tdrecv, afin, tfin, attn, text, wob, gsend, grecv,
                 load_sem, send_sem, x_sem, w_sem, own_sem, kv_sem, q_sem, t_sem, o_sem, r_sem, tr_sem,
                 attn_sem, text_sem, out_sem):
    x, y, z, c = coords()
    zh, zl = z // 2, lax.rem(z, 2)
    role = lax.rem(c + zh, 2)
    is0, is1 = role == 0, role == 1
    sibling = dev(x, y, z, 1 - c)
    partner = dev(x, y, z + 2, 1 - c)
    xp, xm = dev(x + 1, y, z, c), dev(x - 1, y, z, c)
    yps = {1: dev(x, y + 1, z, c), 2: dev(x, y - 1, z, c), 3: dev(x, y + 2, z, c)}
    zp, zm = dev(x, y, z + 1, c), dev(x, y, z - 1, c)

    load_x = pltpu.make_async_copy(x_ref, xb.at[c], load_sem.at[0])
    load_mod = [
        pltpu.make_async_copy(mod_ref.at[pl.ds(2 * i, 2)], part, load_sem.at[1 + i])
        for i, part in enumerate((mod0, mod1, mod2))]
    load_wv = [
        pltpu.make_async_copy(wv_ref.at[part], wvb.at[:, part * W : (part + 1) * W], load_sem.at[4 + part])
        for part in range(3)]
    load_xt = pltpu.make_async_copy(xt_ref, xtb, load_sem.at[7])
    load_wt = [
        pltpu.make_async_copy(wt_ref.at[part], wtb.at[pl.ds(part * D, D)], load_sem.at[8 + part])
        for part in range(3)]
    for copy in [load_x, load_mod[0]] + load_wv:
        copy.start()

    @pl.when(is0)
    def _():
        for copy in [load_xt] + load_wt:
            copy.start()

    load_mod[1].start()
    load_mod[2].start()

    barrier = pltpu.get_barrier_semaphore()
    for device in (sibling, xp, xm, yps[1], yps[2], yps[3], zp, zm, dev(x, y, z + 2, zh)):
        signal(barrier, device)

    @pl.when(is1)
    def _():
        signal(barrier, dev(x, y, z + 2, 1 - zh))

    step = step_ref[0]
    load_x.wait()
    load_mod[0].wait()
    shift, scale1 = mod0[0, pl.ds(step, 1), :], 1.0 + mod0[1, pl.ds(step, 1), :]
    norm_rows(xb.at[c], nb, 128 * c, 128, shift, scale1)
    pl.semaphore_wait(barrier, 9 + role)

    sends = Sends(send_sem, sibling)

    def arrived(dst, sem):
        pltpu.make_async_remote_copy(
            src_ref=dst, dst_ref=dst, send_sem=send_sem.at[0], recv_sem=sem,
            device_id=sibling, device_id_type=MESH).wait_recv()

    for rows, device, sem in ((pl.ds(0, 64), zm, x_sem.at[1]), (pl.ds(64, 64), zp, x_sem.at[2])):
        sends.start(lambda rows=rows: x_ref.at[rows], xb.at[2 + c, rows], sem, device)
    sends.start(x_ref, xb.at[c], x_sem.at[0], sibling)

    def q_half(pos, half):
        return qb.at[pl.ds(q_row(pos, half), HALF)]

    def send_queries(src, half, pred):
        for pos, back in ((3, 3), (1, 2), (2, 1)):
            sends.start(src, q_half(back, half), q_sem.at[back, half], yps[pos], pred)

    def send_keys(src, r, half, pred):
        sends.start(src, kvb.at[r, 2, half], kv_sem.at[r, 2, half, 0], xp, pred)
        sends.start(src, kvb.at[r, 1, half], kv_sem.at[r, 1, half, 0], xm, pred)
        sends.start(src, kvb.at[r, 0, half], kv_sem.at[r, 0, half, 0], sibling, pred)

    def stage_q(half):
        return stg.at[half, 0]

    def stage_kv(half):
        return stg.at[half, pl.ds(1, 2)]

    def send_half(half):
        copies = [
            pltpu.make_async_copy(stage_q(half), q_half(0, half), own_sem.at[half, 0]),
            pltpu.make_async_copy(stage_kv(half), kvb.at[0, 0, half], own_sem.at[half, 1])]
        for copy in copies:
            copy.start()
        send_keys(lambda: stage_kv(half), 0, half, is0)
        if half == 0:
            send_queries(lambda: stage_q(half), half, is0)
        for copy in copies:
            copy.wait()

    def swap_q(half):
        sends.start(lambda: stage_q(half), q_half(0, half), q_sem.at[0, half], partner, is1)

    def swap_kv(half):
        sends.start(lambda: stage_kv(half), kvb.at[1, 0, half], kv_sem.at[1, 0, half, 0], partner, is1)

    def swapped_q(half):
        arrived(q_half(0, half), q_sem.at[0, half])
        send_queries(lambda: q_half(0, half), half, is1)

    def swapped_kv(half):
        arrived(kvb.at[1, 0, half], kv_sem.at[1, 0, half, 0])
        send_keys(lambda: kvb.at[1, 0, half], 1, half, is1)

    def pass_on(r, half, pred):
        arrived(kvb.at[r, 1, half], kv_sem.at[r, 1, half, 0])
        sends.start(lambda: kvb.at[r, 1, half, 0], kvb.at[r, 3, half, 0], kv_sem.at[r, 3, half, 0], xm, pred)
        arrived(kvb.at[r, 2, half], kv_sem.at[r, 2, half, 0])
        sends.start(lambda: kvb.at[r, 2, half, 1], kvb.at[r, 3, half, 1], kv_sem.at[r, 3, half, 1], xp, pred)
        for pos in (1, 2):
            sends.start(lambda pos=pos: kvb.at[r, pos, half], kvb.at[r, pos, half],
                        kv_sem.at[r, pos, half, 0], sibling, pred)

    def pass_last(r, half, pred):
        for part in range(2):
            arrived(kvb.at[r, 3, half, part], kv_sem.at[r, 3, half, part])
        sends.start(lambda: kvb.at[r, 3, half], kvb.at[r, 3, half], kv_sem.at[r, 3, half, 0], sibling, pred)

    def from_sibling(r, blocks):
        for pos, half in blocks:
            arrived(kvb.at[r, pos, half], kv_sem.at[r, pos, half, 0])

    def on(pred, *steps):
        @pl.when(pred)
        def _():
            for step in steps:
                step()

    def over(blocks, q0, count, first=False):
        attend(qb, q0, count, [kvb.at[r, p, f, 0] for r, p, f in blocks],
               [kvb.at[r, p, f, 1] for r, p, f in blocks], acc, first)

    arrived(xb.at[1 - c], x_sem.at[0])
    norm_rows(xb.at[1 - c], nb, 128 * (1 - c), 128, shift, scale1)
    for copy in load_wv:
        copy.wait()
    project_wide(nb[...], wvb, stg.at[0], gains_ref[0:1, :], gains_ref[1:2, :])
    on(is0, lambda: send_half(0))
    on(is1, lambda: swap_q(0))
    ours = pl.ds(pl.multiple_of((2 * zl + c) * W, 16), W)
    theirs = pl.ds(pl.multiple_of((2 * zl + 1 - c) * W, 16), W)
    quarter = W // 4

    def send_weights(piece):
        for side, device in ((0, zp), (1, zm)):
            first_row = (2 * side + piece) * quarter
            place = pl.multiple_of((2 * zl + c) * W + first_row, 16)
            sends.start(lambda first_row=first_row: wov_ref.at[pl.ds(first_row, quarter)],
                        wob.at[pl.ds(place, quarter)], w_sem.at[2 + 2 * side + piece], device)

    def far_piece(core, k):
        return wob.at[pl.ds(pl.multiple_of((2 - 2 * zl + core) * W + k * quarter, 16), quarter)]

    def pass_weights(piece):
        for k in (piece, 2 + piece):
            arrived(far_piece(c, k), w_sem.at[2 + k])
            sends.start(lambda k=k: far_piece(c, k), far_piece(c, k), w_sem.at[6 + k], sibling)

    sends.start(wot_ref, wst_ref, w_sem.at[1], sibling)
    load_wo = pltpu.make_async_copy(wov_ref, wob.at[ours], load_sem.at[11])
    load_wo.start()
    load_mod[1].wait()
    load_mod[2].wait()

    tq_row = pl.multiple_of(64 * x, 64)
    tq_other = tqst.at[pl.ds(pl.multiple_of(64 * x + TQ, TQ), TQ)]
    tq_own = qb.at[pl.ds(TROW, TQ)]

    @pl.when(is0)
    def _():
        load_xt.wait()
        for copy in load_wt:
            copy.wait()
        norm_rows(xtb, nb, 0, TXT, mod1[1, pl.ds(step, 1), :], 1.0 + mod2[0, pl.ds(step, 1), :])
        project(nb[...], [wtb.at[pl.ds(part * D, D)] for part in range(3)],
                [tqst, tkv.at[0], tkv.at[1]], gains_ref[2:3, :], gains_ref[3:4, :])
        copy = pltpu.make_async_copy(tqst.at[pl.ds(tq_row, TQ)], tq_own, own_sem.at[2, 0])
        copy.start()
        sends.start(tq_other, tq_own, t_sem.at[0], sibling, is0)
        sends.start(tkv, tkv, t_sem.at[1], sibling, is0)
        copy.wait()

    arrived(xb.at[2 + c, pl.ds(0, 64)], x_sem.at[1])
    arrived(xb.at[2 + c, pl.ds(64, 64)], x_sem.at[2])
    sends.start(xb.at[2 + c], xb.at[2 + c], x_sem.at[3], sibling)
    on(is1, lambda: swap_kv(0))
    norm_rows(xb.at[2 + c], nb, 128 * c, 128, shift, scale1)
    on(is1, lambda: swapped_q(0))
    arrived(xb.at[3 - c], x_sem.at[3])
    norm_rows(xb.at[3 - c], nb, 128 * (1 - c), 128, shift, scale1)
    on(is0, lambda: pass_on(0, 0, is0))
    project_wide(nb[...], wvb, stg.at[1], gains_ref[0:1, :], gains_ref[1:2, :])
    on(is0, lambda: send_half(1))
    on(is1, lambda: swap_q(1), lambda: swap_kv(1), lambda: swapped_kv(0))

    first_rows = q_row(ORDER[0], 0)

    def rows_of(base, size, i):
        return pl.multiple_of(base + i * size, 16)

    on(is1, lambda: from_sibling(0, [(0, 0), (1, 0), (2, 0)]))
    for pos in (1, 2, 3):
        arrived(q_half(pos, 0), q_sem.at[pos, 0])

    def first(i, carry):
        on(jnp.logical_and(i == 1, is0), lambda: send_queries(lambda: stage_q(1), 1, is0),
           lambda: pass_last(0, 0, is0))
        on(jnp.logical_and(i == 1, is1), lambda: swapped_q(1))
        over([(0, 0, 0), (0, 1, 0), (0, 2, 0)], rows_of(first_rows, 512, i), 512, True)
        return carry

    lax.fori_loop(0, 2, first, 0)
    on(is0, lambda: from_sibling(1, [(0, 0)]))
    on(is1, lambda: from_sibling(0, [(3, 0), (0, 1)]))

    def second(i, carry):
        over([(0, 3, 0), (0, 0, 1), (1, 0, 0)], rows_of(first_rows, 512, i), 512)
        return carry

    lax.fori_loop(0, 2, second, 0)
    on(is0, lambda: pass_on(0, 1, is0))
    on(is1, lambda: pass_on(1, 0, is1),
       lambda: arrived(tq_own, t_sem.at[0]), lambda: arrived(tkv, t_sem.at[1]))
    send_weights(0)

    arrived(wst_ref, w_sem.at[1])
    load_wo_text = []
    for i in range(8):
        cols = slice(i * W, (i + 1) * W)
        for k, (src, place) in enumerate(((wot_ref, c), (wst_ref, 1 - c))):
            rows = pl.ds(pl.multiple_of(i * 2 * W + place * W, 16), W)
            load_wo_text.append(pltpu.make_async_copy(
                src.at[:, cols], wtb.at[rows], load_sem.at[12 + 2 * i + k]))
    for copy in load_wo_text:
        copy.start()
    for pos in (1, 2, 3):
        arrived(q_half(pos, 1), q_sem.at[pos, 1])

    def third(i, carry):
        on(jnp.logical_and(i == 1, is1), lambda: swapped_kv(1))
        over([(0, 0, 0), (0, 1, 0), (0, 2, 0), (0, 3, 0), (0, 0, 1), (1, 0, 0)],
             rows_of(0, 528, i), 528, True)
        return carry

    lax.fori_loop(0, 2, third, 0)
    send_weights(1)
    sends.start(wov_ref, wob.at[ours], w_sem.at[0], sibling)
    on(is1, lambda: pass_last(1, 0, is1),
       lambda: from_sibling(0, [(1, 1), (2, 1)]))
    on(is0, lambda: pass_last(0, 1, is0), lambda: from_sibling(1, [(1, 0), (2, 0), (0, 1)]))

    limit = len_ref[0]
    text_limit = jnp.where(y == 0, limit, 0)
    for q0, count, most in ((TROW, TQ, text_limit), (q_row(0, 1), HALF, limit), (q_row(0, 0), HALF, limit)):
        mask = lax.broadcasted_iota(jnp.int32, (count, TXT), 1) < most
        attend(qb, q0, count, [tkv.at[0]], [tkv.at[1]], acc, False, mask)

    middle_blocks = [(0, 1, 1), (0, 2, 1), (1, 1, 0), (1, 2, 0), (1, 0, 1)]
    last_blocks = [(0, 3, 1), (1, 3, 0), (1, 1, 1), (1, 2, 1), (1, 3, 1)]

    def middle(i, carry):
        on(jnp.logical_and(i == 1, is1), lambda: pass_on(1, 1, is1))
        over(middle_blocks, rows_of(0, 528, i), 528)
        return carry

    lax.fori_loop(0, 2, middle, 0)
    on(is1, lambda: pass_last(1, 1, is1), lambda: from_sibling(0, [(3, 1)]))
    on(is0, lambda: from_sibling(1, [(3, 0), (1, 1), (2, 1), (3, 1)]))

    def fill_sums(pos, half):
        rows = pl.ds(q_row(pos, half), HALF)
        for h in range(NH):
            osend[pos - 1, half, :, h * HD : (h + 1) * HD] = acc[h, rows, :HD].astype(BF16)
        dsend[pos - 1, half] = jnp.transpose(coded_denoms(acc, rows))[:24]

    def send_far(half):
        fill_sums(3, half)
        for part, device in ((0, yps[1]), (1, yps[2])):
            cut = pl.ds(128 * part, 128)
            sends.start(lambda cut=cut: osend.at[2, half, cut], rrecv.at[part, half],
                        r_sem.at[part, half, 0], device)
            sends.start(lambda cut=cut: dsend.at[2, half, :, cut], rden.at[part, half],
                        r_sem.at[part, half, 1], device)

    def send_near(half):
        for pos, part in ((1, 0), (2, 1)):
            back = 1 - part
            fill_sums(pos, half)
            arrived(rrecv.at[part, half], r_sem.at[part, half, 0])
            arrived(rden.at[part, half], r_sem.at[part, half, 1])
            cut = slice(128 * part, 128 * part + 128)
            rows = pl.ds(q_row(pos, half) + 128 * part, 128)
            for h in range(NH):
                lanes = slice(h * HD, (h + 1) * HD)
                osend[pos - 1, half, cut, lanes] = (
                    acc[h, rows, :HD] + rrecv[part, half, :, lanes].astype(F32)).astype(BF16)
            dsend[pos - 1, half, :, cut] = dsend[pos - 1, half, :, cut] + rden[part, half]
            sends.start(lambda pos=pos: osend.at[pos - 1, half], orecv.at[back, half],
                        o_sem.at[back, half, 0], yps[pos])
            sends.start(lambda pos=pos: dsend.at[pos - 1, half], drecv.at[back, half],
                        o_sem.at[back, half, 1], yps[pos])

    acol = pl.ds(pl.multiple_of((2 * zl + zh) * W, HD), W)
    ahead = 1 - 2 * role

    def combine(half):
        for part in range(2):
            arrived(orecv.at[part, half], o_sem.at[part, half, 0])
            arrived(drecv.at[part, half], o_sem.at[part, half, 1])
        rows = pl.ds(q_row(0, half), HALF)
        denoms = drecv[0, half] + drecv[1, half]
        for h in range(NH):
            lanes = slice(h * HD, (h + 1) * HD)
            numer = acc[h, rows, :HD]
            for part in range(2):
                numer = numer + orecv[part, half, :, lanes].astype(F32)
            denom = acc[h, rows, HD:] + jnp.transpose(
                jnp.broadcast_to(denoms[8 * h : 8 * h + 1, :], (HD, HALF)))
            afin[half, :, lanes] = (numer / denom).astype(BF16)
        if half:
            for core in range(2):
                for first_row, step_z in ((0, ahead), (64, -ahead)):
                    rows = pl.ds(core * 128 + first_row, 64)
                    sends.start(lambda rows=rows: afin.at[half, rows],
                                attn.at[pl.ds(first_row, 64), acol], attn_sem.at[1],
                                dev(x, y, z + step_z, core))
            return
        for core in range(2):
            dst = attn.at[:, acol]
            across = jnp.logical_and(is0, c != core)

            def src(core=core):
                return afin.at[0, pl.ds(core * 128, 128)]

            @pl.when(is1)
            def _():
                sends.start(src, dst, attn_sem.at[0], dev(x, y, z + 2, core), is1)

            @pl.when(jnp.logical_and(is0, c == core))
            def _():
                pltpu.make_async_copy(src(), dst, attn_sem.at[0]).start()

            @pl.when(across)
            def _():
                sends.start(src, dst, attn_sem.at[0], sibling, across)

    over(last_blocks, TROW, TQ + HALF)

    trows = pl.ds(TROW, TQ)
    for h in range(NH):
        tsend[:, h * HD : (h + 1) * HD] = acc[h, trows, :HD].astype(BF16)
    tden[...] = coded_denoms(acc, trows)
    for pos, back in ((3, 3), (1, 2), (2, 1)):
        sends.start(tsend, trecv.at[back - 1], tr_sem.at[back - 1, 0], yps[pos])
        sends.start(tden, tdrecv.at[back - 1], tr_sem.at[back - 1, 1], yps[pos])
    send_far(1)
    over(last_blocks, q_row(1, 1), 512)
    over(last_blocks, q_row(0, 1), HALF)
    send_near(1)

    for pos in range(3):
        arrived(trecv.at[pos], tr_sem.at[pos, 0])
        arrived(tdrecv.at[pos], tr_sem.at[pos, 1])
    denoms = tden[...] + tdrecv[0] + tdrecv[1] + tdrecv[2]
    for h in range(NH):
        lanes = slice(h * HD, (h + 1) * HD)
        numer = acc[h, trows, :HD]
        for pos in range(3):
            numer = numer + trecv[pos, :, lanes].astype(F32)
        tfin[:, lanes] = (numer / denoms[:, 8 * h : 8 * h + 1]).astype(BF16)
    place = text.at[pl.ds(pl.multiple_of(lax.rem(x // 2, 2) * 64 + 32 * role, 32), TQ),
                    pl.ds(pl.multiple_of(zh * W, HD), W)]
    core_of = lax.rem(x, 2)
    for dx in range(4):
        for dz in range(2):
            if dx + dz:
                sends.start(tfin, place, text_sem.at[0], dev(x + dx, y, z + 2 * dz, core_of))
    elsewhere = core_of != c

    @pl.when(core_of == c)
    def _():
        pltpu.make_async_copy(tfin, place, text_sem.at[0]).start()

    @pl.when(elsewhere)
    def _():
        sends.start(tfin, place, text_sem.at[0], sibling, elsewhere)

    pass_weights(0)
    over(middle_blocks + last_blocks, q_row(3, 0), HALF)
    send_far(0)
    pass_weights(1)
    over(middle_blocks + last_blocks, q_row(1, 0), 512)
    send_near(0)
    combine(1)

    for copy in load_wo_text:
        copy.wait()
    arrived(text, text_sem.at[0])
    far_row = pl.multiple_of((1 - zl) * 64, 64)
    own_row = pl.multiple_of(zl * 64, 64)
    for i in range(8):
        weight = wtb[i * 2 * W : (i + 1) * 2 * W, :]
        gsend[:, i * W : (i + 1) * W] = jnp.dot(
            text[pl.ds(far_row, 64), :], weight, preferred_element_type=F32).astype(BF16)
    low, high = pl.ds(0, 32), pl.ds(32, 32)
    sends.start(gsend.at[low], grecv.at[low], out_sem.at[0], zp)
    sends.start(gsend.at[high], grecv.at[high], out_sem.at[0], zm)
    over(middle_blocks + last_blocks, q_row(0, 0), HALF)
    combine(0)
    row = lax.broadcasted_iota(jnp.int32, (64, W), 0) + (zl * 2 + c) * 64
    valid = row < len_ref[0]
    for i in range(8):
        cols = slice(i * W, (i + 1) * W)
        weight = wtb[i * 2 * W : (i + 1) * 2 * W, :]
        own = jnp.dot(text[pl.ds(own_row, 64), :], weight, preferred_element_type=F32)
        if i == 0:
            arrived(grecv, out_sem.at[0])
        gate = mod2[1, pl.ds(step, 1), cols]
        text_out_ref[:, cols] = jnp.where(
            valid, gate * (own + grecv[:, cols].astype(F32)), 0.0).astype(BF16)
    load_wo.wait()
    arrived(wob.at[theirs], w_sem.at[0])
    for k in range(4):
        arrived(far_piece(1 - c, k), w_sem.at[6 + k])
    for part, group in ((1, 1 - zl), (0, zl)):
        arrived(attn.at[:, pl.ds(pl.multiple_of(group * 2 * W, HD), 2 * W)], attn_sem.at[part])
    for i in range(NCH):
        cols = slice(i * CH, (i + 1) * CH)
        out = jnp.dot(attn[...], wob[:, cols], preferred_element_type=F32)
        video_out_ref[:, cols] = (mod1[0, pl.ds(step, 1), cols] * out).astype(BF16)
    sends.finish()


def place_kernel(video_ref, text_ref, video_out_ref, text_out_ref):
    video_out_ref[...] = video_ref[...]
    text_out_ref[...] = text_ref[...]


ANY = pl.BlockSpec(memory_space=pl.ANY)
VMEM = pl.BlockSpec(memory_space=pltpu.VMEM)
SMEM = pl.BlockSpec(memory_space=pltpu.SMEM)
DMA = pltpu.SemaphoreType.DMA


def body(x_video, x_text, w_qkv_video, w_qkv_text, w_out_video, w_out_text, qk_gains, modulation,
         text_len, timestep):
    wv = jnp.transpose(w_qkv_video, (1, 0, 2))
    wt = jnp.transpose(w_qkv_text, (1, 0, 2))
    mod = jnp.transpose(modulation, (1, 0, 2))
    shape = jax.ShapeDtypeStruct
    steps = modulation.shape[0]
    results = [shape((128, D), BF16), shape((64, D), BF16)]
    video, text, unused = pl.pallas_call(
        block_kernel,
        name="block",
        in_specs=[ANY, ANY, ANY, ANY, ANY, VMEM, ANY, ANY, SMEM, SMEM],
        out_specs=[VMEM, VMEM, ANY],
        out_shape=results + [shape((W, D), BF16)],
        scratch_shapes=[
            pltpu.VMEM((4, 128, D), BF16), pltpu.VMEM((TXT, D), BF16),
            pltpu.VMEM((D, 3 * W), BF16), pltpu.VMEM((3 * D, W), BF16),
            pltpu.VMEM((2, steps, D), F32), pltpu.VMEM((2, steps, D), F32), pltpu.VMEM((2, steps, D), F32),
            pltpu.VMEM((HALF, D), BF16),
            pltpu.VMEM((2, 3, HALF, W), BF16), pltpu.VMEM((TXT, W), BF16),
            pltpu.VMEM((QROWS, W), BF16), pltpu.VMEM((2, 4, 2, 2, HALF, W), BF16),
            pltpu.VMEM((2, TXT, W), BF16), pltpu.VMEM((NH, QROWS, 2 * HD), F32),
            pltpu.VMEM((3, 2, HALF, W), BF16), pltpu.VMEM((3, 2, 24, HALF), F32),
            pltpu.VMEM((2, 2, HALF, W), BF16), pltpu.VMEM((2, 2, 24, HALF), F32),
            pltpu.VMEM((2, 2, 128, W), BF16), pltpu.VMEM((2, 2, 24, 128), F32),
            pltpu.VMEM((TQ, W), BF16), pltpu.VMEM((TQ, HD), F32),
            pltpu.VMEM((3, TQ, W), BF16), pltpu.VMEM((3, TQ, HD), F32),
            pltpu.VMEM((2, HALF, W), BF16), pltpu.VMEM((TQ, W), BF16),
            pltpu.VMEM((128, 4 * W), BF16), pltpu.VMEM((128, 2 * W), BF16), pltpu.VMEM((4 * W, D), BF16),
            pltpu.VMEM((64, D), BF16), pltpu.VMEM((64, D), BF16),
            DMA((28,)), DMA((136,)), DMA((4,)), DMA((10,)), DMA((3, 2)), DMA((2, 4, 2, 2)), DMA((4, 2)),
            DMA((2,)), DMA((2, 2, 2)), DMA((2, 2, 2)), DMA((3, 2)), DMA((2,)), DMA((1,)), DMA((1,))],
        compiler_params=pltpu.CompilerParams(
            collective_id=1, has_side_effects=True, vmem_limit_bytes=VMEM_LIMIT),
    )(x_video, x_text, wv, wt, mod, qk_gains, w_out_video, w_out_text, text_len, timestep)
    return tuple(pl.pallas_call(
        place_kernel,
        name="place",
        in_specs=[VMEM, VMEM],
        out_specs=[VMEM, VMEM],
        out_shape=results,
    )(video, text))


def solution(mesh):
    grid = Mesh(mesh.devices.reshape(4, 4, 2, 2, 2), AXES)
    head = ("zl", "c")
    return jax.shard_map(
        body,
        mesh=grid,
        in_specs=(P(AXES, None), P(), P(None, None, head), P(None, None, head),
                  P(head, None), P(head, None), P(), P(), P(), P()),
        out_specs=(P(AXES, None), P(head, None)),
        check_vma=False,
    )
```

profile of v0, /device:TPU:1, one launch (start us, length us, event | category | flops | bytes accessed | tf_op | source)
XLA Modules:
  0.0 93.1 jit_solution(17669661165985089493)
XLA Ops:
  1.9 88.9 %block.1 = (bf16[128,3072]{1,0:T(8,128)(2,1)}, bf16[64,3072]{1,0:T(8,128)(2,1)}, bf16[384,3072]{1,0:T(8,128)(2,1)}) custom-call(bf16[128,3072]{1,0:T(8,128)(2,1)} %x_ref.1, bf16[256,3072]{1,0:T(8,128)(2,1)} %xt_ref.1, bf16[3,3072,384]{2,1,0:T(8,128)(2,1)} %bitcast.3, bf16[3,3072,384]{2,1,0:T(8,128)(2,1)} %bitcast.4, f32[6,50,3072]{2,1,0:T(8,128)} %bitcast.5, ...), custom_call_target="tpu_custom_call" | custom-call | tf_op jit(solution)/shard_map/block/pallas_call | solution.py:598
  90.8 2.3 %place.1 = (bf16[128,3072]{1,0:T(8,128)(2,1)}, bf16[64,3072]{1,0:T(8,128)(2,1)}) custom-call(bf16[128,3072]{1,0:T(8,128)(2,1)} %get-tuple-element.4.video_ref, bf16[64,3072]{1,0:T(8,128)(2,1)} %get-tuple-element.5.text_ref), custom_call_target="tpu_custom_call" | custom-call | tf_op jit(solution)/shard_map/place/pallas_call | solution.py:625
where the time goes:
time: 93.3 us; the launch traced here: 93.1 us
  Pallas kernels  91.2 us (98%)
  between operations  1.93 us (2%)
    pallas_call x1, Pallas kernels, body(): pl.pallas_call(block_kernel, name='block', in_specs=[ANY, ANY, ANY, ANY,...  88.9 us
    pallas_call x1, Pallas kernels, body(): pl.pallas_call(place_kernel, name='place', in_specs=[VMEM, VMEM], out_spe...  2.29 us

commit v1 on v0

--- a/solution.py
+++ b/solution.py
@@ -142,7 +142,7 @@
 def block_kernel(x_ref, xt_ref, wv_ref, wt_ref, mod_ref, gains_ref, wov_ref, wot_ref, len_ref, step_ref,
                  video_out_ref, text_out_ref, wst_ref,
                  xb, xtb, wvb, wtb, mod0, mod1, mod2, nb, stg, tqst, qb, kvb, tkv, acc, osend, dsend, orecv, drecv,
-                 rrecv, rden, tsend, tden, trecv, tdrecv, afin, tfin, attn, text, wob, gsend, grecv,
+                 rrecv, rden, tsend, tden, trecv, tdrecv, afin, tfin, attn, text, wob, gsend, grecv, gown, vown,
                  load_sem, send_sem, x_sem, w_sem, own_sem, kv_sem, q_sem, t_sem, o_sem, r_sem, tr_sem,
                  attn_sem, text_sem, out_sem):
     x, y, z, c = coords()
@@ -533,7 +533,6 @@
     pass_weights(0)
     over(middle_blocks + last_blocks, q_row(3, 0), HALF)
     send_far(0)
-    pass_weights(1)
     over(middle_blocks + last_blocks, q_row(1, 0), 512)
     send_near(0)
     combine(1)
@@ -550,29 +549,40 @@
     low, high = pl.ds(0, 32), pl.ds(32, 32)
     sends.start(gsend.at[low], grecv.at[low], out_sem.at[0], zp)
     sends.start(gsend.at[high], grecv.at[high], out_sem.at[0], zm)
+    pass_weights(1)
     over(middle_blocks + last_blocks, q_row(0, 0), HALF)
     combine(0)
-    row = lax.broadcasted_iota(jnp.int32, (64, W), 0) + (zl * 2 + c) * 64
-    valid = row < len_ref[0]
+
     for i in range(8):
-        cols = slice(i * W, (i + 1) * W)
         weight = wtb[i * 2 * W : (i + 1) * 2 * W, :]
-        own = jnp.dot(text[pl.ds(own_row, 64), :], weight, preferred_element_type=F32)
-        if i == 0:
-            arrived(grecv, out_sem.at[0])
-        gate = mod2[1, pl.ds(step, 1), cols]
-        text_out_ref[:, cols] = jnp.where(
-            valid, gate * (own + grecv[:, cols].astype(F32)), 0.0).astype(BF16)
+        gown[:, i * W : (i + 1) * W] = jnp.dot(
+            text[pl.ds(own_row, 64), :], weight, preferred_element_type=F32)
     load_wo.wait()
     arrived(wob.at[theirs], w_sem.at[0])
     for k in range(4):
         arrived(far_piece(1 - c, k), w_sem.at[6 + k])
-    for part, group in ((1, 1 - zl), (0, zl)):
-        arrived(attn.at[:, pl.ds(pl.multiple_of(group * 2 * W, HD), 2 * W)], attn_sem.at[part])
+
+    def product(group, cols):
+        rows = pl.ds(pl.multiple_of(group * 2 * W, HD), 2 * W)
+        return jnp.dot(attn[:, rows], wob[rows, cols], preferred_element_type=F32)
+
+    arrived(attn.at[:, pl.ds(pl.multiple_of((1 - zl) * 2 * W, HD), 2 * W)], attn_sem.at[1])
     for i in range(NCH):
         cols = slice(i * CH, (i + 1) * CH)
-        out = jnp.dot(attn[...], wob[:, cols], preferred_element_type=F32)
-        video_out_ref[:, cols] = (mod1[0, pl.ds(step, 1), cols] * out).astype(BF16)
+        vown[:, cols] = product(1 - zl, cols)
+    arrived(attn.at[:, pl.ds(pl.multiple_of(zl * 2 * W, HD), 2 * W)], attn_sem.at[0])
+    for i in range(NCH):
+        cols = slice(i * CH, (i + 1) * CH)
+        video_out_ref[:, cols] = (
+            mod1[0, pl.ds(step, 1), cols] * (vown[:, cols] + product(zl, cols))).astype(BF16)
+    arrived(grecv, out_sem.at[0])
+    row = lax.broadcasted_iota(jnp.int32, (64, CH), 0) + (zl * 2 + c) * 64
+    valid = row < len_ref[0]
+    for i in range(NCH):
+        cols = slice(i * CH, (i + 1) * CH)
+        text_out_ref[:, cols] = jnp.where(
+            valid, mod2[1, pl.ds(step, 1), cols] * (gown[:, cols] + grecv[:, cols].astype(F32)),
+            0.0).astype(BF16)
     sends.finish()
 
 
@@ -617,6 +627,7 @@
             pltpu.VMEM((2, HALF, W), BF16), pltpu.VMEM((TQ, W), BF16),
             pltpu.VMEM((128, 4 * W), BF16), pltpu.VMEM((128, 2 * W), BF16), pltpu.VMEM((4 * W, D), BF16),
             pltpu.VMEM((64, D), BF16), pltpu.VMEM((64, D), BF16),
+            pltpu.VMEM((64, D), F32), pltpu.VMEM((128, D), F32),
             DMA((28,)), DMA((136,)), DMA((4,)), DMA((10,)), DMA((3, 2)), DMA((2, 4, 2, 2)), DMA((4, 2)),
             DMA((2,)), DMA((2, 2, 2)), DMA((2, 2, 2)), DMA((3, 2)), DMA((2,)), DMA((1,)), DMA((1,))],
         compiler_params=pltpu.CompilerParams(

time: 93.3 us -> 92.8 us (level)
  no operation moved by 1% of the time
where the time goes in v1:
time: 92.8 us; the launch traced here: 92.6 us
  Pallas kernels  90.7 us (98%)
  between operations  1.93 us (2%)
    pallas_call x1, Pallas kernels, body(): pl.pallas_call(block_kernel, name='block', in_specs=[ANY, ANY, ANY, ANY,...  88.4 us
    pallas_call x1, Pallas kernels, body(): pl.pallas_call(place_kernel, name='place', in_specs=[VMEM, VMEM], out_spe...  2.29 us

profile of v1, /device:TPU:1, one launch (start us, length us, event | category | flops | bytes accessed | tf_op | source)
XLA Modules:
  0.0 92.6 jit_solution(8283150499225522606)
XLA Ops:
  1.9 88.4 %block.1 = (bf16[128,3072]{1,0:T(8,128)(2,1)}, bf16[64,3072]{1,0:T(8,128)(2,1)}, bf16[384,3072]{1,0:T(8,128)(2,1)}) custom-call(bf16[128,3072]{1,0:T(8,128)(2,1)} %x_ref.1, bf16[256,3072]{1,0:T(8,128)(2,1)} %xt_ref.1, bf16[3,3072,384]{2,1,0:T(8,128)(2,1)} %bitcast.3, bf16[3,3072,384]{2,1,0:T(8,128)(2,1)} %bitcast.4, f32[6,50,3072]{2,1,0:T(8,128)} %bitcast.5, ...), custom_call_target="tpu_custom_call" | custom-call | tf_op jit(solution)/shard_map/block/pallas_call | solution.py:608
  90.4 2.3 %place.1 = (bf16[128,3072]{1,0:T(8,128)(2,1)}, bf16[64,3072]{1,0:T(8,128)(2,1)}) custom-call(bf16[128,3072]{1,0:T(8,128)(2,1)} %get-tuple-element.4.video_ref, bf16[64,3072]{1,0:T(8,128)(2,1)} %get-tuple-element.5.text_ref), custom_call_target="tpu_custom_call" | custom-call | tf_op jit(solution)/shard_map/place/pallas_call | solution.py:636

commit v2 on v1

--- a/solution.py
+++ b/solution.py
@@ -364,7 +364,7 @@
 
     lax.fori_loop(0, 2, second, 0)
     on(is0, lambda: pass_on(0, 1, is0))
-    on(is1, lambda: pass_on(1, 0, is1),
+    on(is1, lambda: pass_on(1, 0, is1), lambda: swapped_kv(1),
        lambda: arrived(tq_own, t_sem.at[0]), lambda: arrived(tkv, t_sem.at[1]))
     send_weights(0)
 
@@ -382,7 +382,6 @@
         arrived(q_half(pos, 1), q_sem.at[pos, 1])
 
     def third(i, carry):
-        on(jnp.logical_and(i == 1, is1), lambda: swapped_kv(1))
         over([(0, 0, 0), (0, 1, 0), (0, 2, 0), (0, 3, 0), (0, 0, 1), (1, 0, 0)],
              rows_of(0, 528, i), 528, True)
         return carry
@@ -403,8 +402,9 @@
     middle_blocks = [(0, 1, 1), (0, 2, 1), (1, 1, 0), (1, 2, 0), (1, 0, 1)]
     last_blocks = [(0, 3, 1), (1, 3, 0), (1, 1, 1), (1, 2, 1), (1, 3, 1)]
 
+    on(is1, lambda: pass_on(1, 1, is1))
+
     def middle(i, carry):
-        on(jnp.logical_and(i == 1, is1), lambda: pass_on(1, 1, is1))
         over(middle_blocks, rows_of(0, 528, i), 528)
         return carry
 

time: 92.8 us -> 91.1 us (0.982)
  Pallas kernels: 90.7 us -> 89 us
    pallas_call x1, Pallas kernels: 88.4 us -> 86.7 us  [body(): pl.pallas_call(block_kernel, name='block', in_specs=[ANY, ANY, ANY, ANY,...]
where the time goes in v2:
time: 91.1 us; the launch traced here: 90.9 us
  Pallas kernels  89 us (98%)
  between operations  1.93 us (2%)
    pallas_call x1, Pallas kernels, body(): pl.pallas_call(block_kernel, name='block', in_specs=[ANY, ANY, ANY, ANY,...  86.7 us
    pallas_call x1, Pallas kernels, body(): pl.pallas_call(place_kernel, name='place', in_specs=[VMEM, VMEM], out_spe...  2.29 us

profile of v2, /device:TPU:1, one launch (start us, length us, event | category | flops | bytes accessed | tf_op | source)
XLA Modules:
  0.0 90.9 jit_solution(472080793026345122)
XLA Ops:
  1.9 86.7 %block.1 = (bf16[128,3072]{1,0:T(8,128)(2,1)}, bf16[64,3072]{1,0:T(8,128)(2,1)}, bf16[384,3072]{1,0:T(8,128)(2,1)}) custom-call(bf16[128,3072]{1,0:T(8,128)(2,1)} %x_ref.1, bf16[256,3072]{1,0:T(8,128)(2,1)} %xt_ref.1, bf16[3,3072,384]{2,1,0:T(8,128)(2,1)} %bitcast.3, bf16[3,3072,384]{2,1,0:T(8,128)(2,1)} %bitcast.4, f32[6,50,3072]{2,1,0:T(8,128)} %bitcast.5, ...), custom_call_target="tpu_custom_call" | custom-call | tf_op jit(solution)/shard_map/block/pallas_call | solution.py:608
  88.6 2.3 %place.1 = (bf16[128,3072]{1,0:T(8,128)(2,1)}, bf16[64,3072]{1,0:T(8,128)(2,1)}) custom-call(bf16[128,3072]{1,0:T(8,128)(2,1)} %get-tuple-element.4.video_ref, bf16[64,3072]{1,0:T(8,128)(2,1)} %get-tuple-element.5.text_ref), custom_call_target="tpu_custom_call" | custom-call | tf_op jit(solution)/shard_map/place/pallas_call | solution.py:636

commit v3 on v2

--- a/solution.py
+++ b/solution.py
@@ -405,11 +405,12 @@
     on(is1, lambda: pass_on(1, 1, is1))
 
     def middle(i, carry):
+        on(jnp.logical_and(i == 1, is1), lambda: pass_last(1, 1, is1))
         over(middle_blocks, rows_of(0, 528, i), 528)
         return carry
 
     lax.fori_loop(0, 2, middle, 0)
-    on(is1, lambda: pass_last(1, 1, is1), lambda: from_sibling(0, [(3, 1)]))
+    on(is1, lambda: from_sibling(0, [(3, 1)]))
     on(is0, lambda: from_sibling(1, [(3, 0), (1, 1), (2, 1), (3, 1)]))
 
     def fill_sums(pos, half):

time: 91.1 us -> 89.8 us (0.986)
  Pallas kernels: 89 us -> 87.7 us
    pallas_call x1, Pallas kernels: 86.7 us -> 85.4 us  [body(): pl.pallas_call(block_kernel, name='block', in_specs=[ANY, ANY, ANY, ANY,...]
where the time goes in v3:
time: 89.8 us; the launch traced here: 89.7 us
  Pallas kernels  87.7 us (98%)
  between operations  1.93 us (2%)
    pallas_call x1, Pallas kernels, body(): pl.pallas_call(block_kernel, name='block', in_specs=[ANY, ANY, ANY, ANY,...  85.4 us
    pallas_call x1, Pallas kernels, body(): pl.pallas_call(place_kernel, name='place', in_specs=[VMEM, VMEM], out_spe...  2.29 us

profile of v3, /device:TPU:1, one launch (start us, length us, event | category | flops | bytes accessed | tf_op | source)
XLA Modules:
  0.0 89.7 jit_solution(13396130064712339521)
XLA Ops:
  1.9 85.4 %block.1 = (bf16[128,3072]{1,0:T(8,128)(2,1)}, bf16[64,3072]{1,0:T(8,128)(2,1)}, bf16[384,3072]{1,0:T(8,128)(2,1)}) custom-call(bf16[128,3072]{1,0:T(8,128)(2,1)} %x_ref.1, bf16[256,3072]{1,0:T(8,128)(2,1)} %xt_ref.1, bf16[3,3072,384]{2,1,0:T(8,128)(2,1)} %bitcast.3, bf16[3,3072,384]{2,1,0:T(8,128)(2,1)} %bitcast.4, f32[6,50,3072]{2,1,0:T(8,128)} %bitcast.5, ...), custom_call_target="tpu_custom_call" | custom-call | tf_op jit(solution)/shard_map/block/pallas_call | solution.py:609
  87.4 2.3 %place.1 = (bf16[128,3072]{1,0:T(8,128)(2,1)}, bf16[64,3072]{1,0:T(8,128)(2,1)}) custom-call(bf16[128,3072]{1,0:T(8,128)(2,1)} %get-tuple-element.4.video_ref, bf16[64,3072]{1,0:T(8,128)(2,1)} %get-tuple-element.5.text_ref), custom_call_target="tpu_custom_call" | custom-call | tf_op jit(solution)/shard_map/place/pallas_call | solution.py:637
